TPU v7x, 128 devices: a whole 4x4x4 slice. The times are simulated.
128 devices in a mesh: clu: 8 (over z, core), row: 16 (over y, x).
Axes of the slice: x: 4, y: 4, z: 4, core: 2. Of those that a mesh axis runs over, the one named last changes fastest.
Arguments:
- rhs: float32 [256, 524288], P(None, ('clu', 'row')), may hold values from -6 to 6
- linv: float32 [2048, 256, 256], P(('clu', 'row'))
- w_one: float32 [524288, 128], P(('clu', 'row')), may hold values from -1.5 to 1.5
- w_two: float32 [524288, 128], P(('clu', 'row')), may hold values from -1.5 to 1.5
- held: int32 [16], replicated, may hold values from 0 to 15, each once
- ranks: int32 [12], replicated, may hold values from 16 to 128, as said below
Outputs:
- solved: float32 [256, 524288], P(None, ('clu', 'row'))
Inputs may be any that keep to these rules, and one draw needn't show every extreme that they name: `ranks`: entries 0 to 7 are the level-one blocks of subtrees in order (two a subtree), the rest the level-two blocks; some entry equals 128. `held`: a permutation of the clusters.
All inputs are finite; a program needn't handle non-finite values.
Results may differ from a plain program's by a relative error of at most 0.0001.
Values sent between devices are 32-bit elements; how exact they have to be, the bound alone decides.
No kernel may reach another device: no remote copies, remote signals or barrier semaphores. Data moves between devices by JAX's collectives and lax.ppermute only.
A program may use at most 128 MiB of HBM per device.

v0:
```python
import math

import jax
import jax.numpy as jnp
from jax import lax
from jax.sharding import PartitionSpec as P


def leaf_apply(values, inverse):
    blocks = inverse.shape[0]
    leaf_width = inverse.shape[1]
    pieces = values.reshape(values.shape[0], blocks, leaf_width).transpose(1, 0, 2)
    result = jnp.einsum("bcj,bij->bci", pieces, inverse, precision=lax.Precision.HIGHEST)
    return result.transpose(1, 0, 2).reshape(values.shape[0], blocks * leaf_width)


def shards(rhs, linv, w_one, w_two, held, ranks):
    highest = lax.Precision.HIGHEST
    local_rows = rhs.shape[1]
    clu_count = lax.axis_size("clu")
    row_count = lax.axis_size("row")
    half_rows = row_count // 2
    slot_count = 2 * clu_count
    tree_count = slot_count // 4
    rank_width = w_one.shape[1]
    scaling = 1.0 / math.sqrt(local_rows * half_rows)
    group_index = lax.axis_index("clu")
    row_index = lax.axis_index("row")
    upper_half = (row_index >= half_rows).astype(jnp.int32)
    own_slot = 2 * group_index + upper_half
    slot_ids = jnp.arange(slot_count)
    own_flag = slot_ids == own_slot
    own_weights = own_flag.astype(jnp.float32)
    own_cluster = jnp.sum(jnp.where(own_flag, held, 0))
    position = own_cluster % 4
    subtree = own_cluster // 4
    tree_weights = (jnp.arange(tree_count) == subtree).astype(jnp.float32)

    def chooser(offset):
        return (held == 4 * subtree + offset).astype(jnp.float32)

    block_ids = jnp.arange(ranks.shape[0])

    def mask_for(block_index):
        rank_value = jnp.sum(jnp.where(block_ids == block_index, ranks, 0))
        return (jnp.arange(rank_width) < rank_value).astype(jnp.float32)

    selector_one = chooser(0)
    selector_two = chooser(0) + chooser(1)
    selector_three = chooser(2)
    mask_one = mask_for(2 * subtree)
    mask_two = mask_for(slot_count // 2 + subtree)
    mask_three = mask_for(2 * subtree + 1)
    flag_one = (position == 1).astype(jnp.float32)
    flag_late = (position >= 2).astype(jnp.float32)
    flag_last = (position == 3).astype(jnp.float32)

    def couple(local_term, selector, rank_mask):
        share = jnp.sum(selector * own_weights)
        slotted = tree_weights[:, None, None] * (local_term * share)[None]
        summed_trees = lax.psum(slotted, ("clu", "row"))
        picked = jnp.einsum("g,gck->ck", tree_weights, summed_trees, precision=highest)
        return picked * rank_mask[None, :]

    current = rhs
    solved = leaf_apply(current, linv)
    coef_one = couple(jnp.dot(solved, w_one, precision=highest) * scaling, selector_one, mask_one)
    current = current - flag_one * jnp.dot(coef_one, w_one.T, precision=highest)
    solved = leaf_apply(current, linv)
    coef_two = couple(jnp.dot(solved, w_two, precision=highest) * scaling, selector_two, mask_two)
    current = current - flag_late * jnp.dot(coef_two, w_two.T, precision=highest)
    solved = leaf_apply(current, linv)
    coef_three = couple(
        jnp.dot(solved, w_one, precision=highest) * scaling, selector_three, mask_three
    )
    current = current - flag_last * jnp.dot(coef_three, w_one.T, precision=highest)
    solved = leaf_apply(current, linv)
    return solved


def solution(mesh):
    in_specs = (
        P(None, ("clu", "row")),
        P(("clu", "row"), None, None),
        P(("clu", "row"), None),
        P(("clu", "row"), None),
        P(),
        P(),
    )
    out_specs = P(None, ("clu", "row"))
    return jax.shard_map(shards, mesh=mesh, in_specs=in_specs, out_specs=out_specs, check_vma=False)
```

profile of v0, /device:TPU:1, one launch (start us, length us, event | category | flops | bytes accessed | tf_op | source)
XLA Modules:
  0.0 537.2 jit_solution(15307076161341010976)
XLA Ops:
  6.5 1.4 select_reduce_fusion.1
  10.6 1.4 fusion.31
  12.6 12.0 %fusion.9 = f32[16,256,256]{1,2,0:T(8,128)S(1)} fusion(f32[16,256,256]{2,1,0:T(8,128)} %param.7, f32[32,16,8,256]{3,2,1,0:T(8,128)} %bitcast.70), kind=kOutput, calls=%fused_computation.16 | convolution fusion | flops 3221225472 | bytes 12582912 | tf_op jit(solution)/shard_map/bcj,bij->bci/dot_general | solution.py:13
  24.7 6.7 %convolution_multiply_fusion.5 = f32[256,128]{1,0:T(8,128)S(1)} fusion(f32[256,4096]{0,1:T(8,128)S(1)} %bitcast.72, f32[4096,128]{1,0:T(8,128)S(1)} %copy-done, f32[]{:T(128)S(6)} %mul.131), kind=kOutput, calls=%fused_computation.20 | convolution fusion | flops 1610645504 | bytes 6422532 | tf_op jit(solution)/shard_map/dot_general | solution.py:67
  31.4 0.9 broadcast_multiply_fusion.2
  33.3 0.7 fusion.32
  34.7 146.2 %all-reduce.4.cloned.1.call-done = f32[4,256,128]{2,1,0:T(8,128)} async-done(((f32[4,256,128]{2,1,0:T(8,128)}), f32[4,256,128]{2,1,0:T(8,128)}) %all-reduce.4.cloned.1.call-update) | async-done | bytes 524304 | tf_op jit(solution)/shard_map/psum | solution.py:61
  180.9 1.9 fusion.15
  182.9 5.6 %fusion.2 = f32[256,4096]{1,0:T(8,128)S(1)} fusion(f32[256,4096]{1,0:T(8,128)} %param.6, f32[4096,128]{1,0:T(8,128)S(1)} %copy-done, f32[]{:T(128)S(6)} %convert_element_type.52, f32[256,128]{1,0:T(8,128)S(1)} %bitcast.78, f32[128]{0:T(128)S(1)} %compare_convert_fusion.4), kind=kOutput, calls=%fused_computation.5 | convolution fusion | flops 1612742656 | bytes 10617348 | tf_op jit(solution)/shard_map/dot_general | solution.py:68
  188.6 5.3 fusion.7
  193.9 6.7 %convolution_multiply_fusion.4 = f32[256,128]{1,0:T(8,128)S(1)} fusion(f32[256,4096]{0,1:T(8,128)S(1)} %bitcast.73, f32[4096,128]{1,0:T(8,128)S(1)} %copy-done.6, f32[]{:T(128)S(6)} %mul.142), kind=kOutput, calls=%fused_computation.19 | convolution fusion | flops 1610645504 | bytes 6422532 | tf_op jit(solution)/shard_map/dot_general | solution.py:70
  200.6 0.9 broadcast_multiply_fusion.1
  203.0 142.5 %all-reduce.6.cloned.1.call-done = f32[4,256,128]{2,1,0:T(8,128)} async-done(((f32[4,256,128]{2,1,0:T(8,128)}), f32[4,256,128]{2,1,0:T(8,128)}) %all-reduce.6.cloned.1.call-update) | async-done | bytes 524304 | tf_op jit(solution)/shard_map/psum | solution.py:61
  345.5 1.9 fusion.13
  347.5 6.5 %fusion.1 = f32[256,4096]{1,0:T(8,128)S(1)} fusion(f32[256,4096]{1,0:T(8,128)} %copy-done.4, f32[4096,128]{1,0:T(8,128)} %param.9, f32[]{:T(128)S(6)} %convert_element_type.56, f32[256,128]{1,0:T(8,128)S(1)} %bitcast.77, f32[128]{0:T(128)S(1)} %compare_convert_fusion.2), kind=kOutput, calls=%fused_computation.3 | convolution fusion | flops 1612742656 | bytes 10617348 | tf_op jit(solution)/shard_map/dot_general | solution.py:71
  354.0 5.3 fusion.5
  359.3 6.7 %convolution_multiply_fusion.3 = f32[256,128]{1,0:T(8,128)S(1)} fusion(f32[256,4096]{0,1:T(8,128)S(1)} %bitcast.74, f32[4096,128]{1,0:T(8,128)S(1)} %copy-done, f32[]{:T(128)S(6)} %mul.152), kind=kOutput, calls=%fused_computation.18 | convolution fusion | flops 1610645504 | bytes 6422532 | tf_op jit(solution)/shard_map/dot_general | solution.py:74
  366.0 0.9 broadcast_multiply_fusion
  367.0 0.7 compare_convert_fusion
  367.7 143.3 %all-reduce.8.cloned.1.call-done = f32[4,256,128]{2,1,0:T(8,128)} async-done(((f32[4,256,128]{2,1,0:T(8,128)}), f32[4,256,128]{2,1,0:T(8,128)}) %all-reduce.8.cloned.1.call-update) | async-done | bytes 524304 | tf_op jit(solution)/shard_map/psum | solution.py:61
  510.9 2.2 fusion.11
  513.2 5.6 %fusion = f32[256,4096]{1,0:T(8,128)S(1)} fusion(f32[256,4096]{1,0:T(8,128)} %copy-done.5, f32[4096,128]{1,0:T(8,128)S(1)} %copy-done, f32[]{:T(128)S(6)} %convert_element_type.59, f32[256,128]{1,0:T(8,128)S(1)} %bitcast.76, f32[128]{0:T(128)S(1)} %compare_convert_fusion), kind=kOutput, calls=%fused_computation.1 | convolution fusion | flops 1612742656 | bytes 10617348 | tf_op jit(solution)/shard_map/dot_general | solution.py:76
  518.8 5.8 %fusion.3 = f32[16,256,256]{1,2,0:T(8,128)} fusion(f32[16,256,256]{2,1,0:T(8,128)S(1)} %copy-done.3, f32[32,16,8,256]{3,2,1,0:T(8,128)S(1)} %bitcast.71), kind=kOutput, calls=%fused_computation.7 | convolution fusion | flops 3221225472 | bytes 12582912 | tf_op jit(solution)/shard_map/bcj,bij->bci/dot_general | solution.py:13
  524.7 5.6 %copy.11 = f32[256,4096]{1,0:T(8,128)} copy(f32[256,4096]{0,1:T(8,128)} %bitcast.75) | data formatting | bytes 8388608 | tf_op jit(solution)/shard_map/reshape | solution.py:14
  (25 shorter events, 1.9 us)
Async XLA Ops:
  6.5 18.1 %copy-start = (f32[4096,128]{1,0:T(8,128)S(1)}, f32[4096,128]{1,0:T(8,128)}, u32[]{:S(2)}) copy-start(f32[4096,128]{1,0:T(8,128)} %param.8) | copy-start | bytes 6291460
  6.5 174.4 %all-reduce.4.cloned.1.call-start = ((), (), s32[]{:S(2)}) async-start(), calls=%async_computation | async-start | bytes 1048576 | tf_op jit(solution)/shard_map/psum | solution.py:61
  24.6 8.6 %copy-start.7 = (s32[12]{0:T(128)S(1)}, s32[12]{0:T(128)}, u32[]{:S(2)}) copy-start(s32[12]{0:T(128)} %param.11) | copy-start | bytes 148
  32.3 313.2 %all-reduce.6.cloned.1.call-start = ((), (), s32[]{:S(2)}) async-start(), calls=%async_computation.1 | async-start | bytes 1048576 | tf_op jit(solution)/shard_map/psum | solution.py:61
  182.9 5.7 %copy-start.1 = (f32[16,256,256]{2,1,0:T(8,128)S(1)}, f32[16,256,256]{2,1,0:T(8,128)}, u32[]{:S(2)}) copy-start(f32[16,256,256]{2,1,0:T(8,128)} %param.7) | copy-start | bytes 12582916
  188.5 5.3 copy-start.4
  188.5 5.3 copy-start.6
  201.6 309.4 %all-reduce.8.cloned.1.call-start = ((), (), s32[]{:S(2)}) async-start(), calls=%async_computation.2 | async-start | bytes 1048576 | tf_op jit(solution)/shard_map/psum | solution.py:61
  347.4 6.5 %copy-start.2 = (f32[16,256,256]{2,1,0:T(8,128)S(1)}, f32[16,256,256]{2,1,0:T(8,128)}, u32[]{:S(2)}) copy-start(f32[16,256,256]{2,1,0:T(8,128)} %param.7) | copy-start | bytes 12582916
  353.9 5.3 copy-start.5
  513.1 5.7 %copy-start.3 = (f32[16,256,256]{2,1,0:T(8,128)S(1)}, f32[16,256,256]{2,1,0:T(8,128)}, u32[]{:S(2)}) copy-start(f32[16,256,256]{2,1,0:T(8,128)} %param.7) | copy-start | bytes 12582916
Sparse Core Ops, SparseCore 0:
  32.4 148.4 all-reduce.3
  201.7 143.7 all-reduce.5
  367.1 143.8 all-reduce.7
where the time goes:
time: 545 us; the launch traced here: 537 us
  waiting for transfers between devices  432 us (79%)
  matrix products  72.5 us (13%)
  between operations  18.3 us (3%)
  other arithmetic  8.26 us (2%)
  local copies, waits for them, and re-layouts  5.64 us (1%)
    psum x3, waiting for transfers between devices, couple(): summed_trees = lax.psum(slotted, ('clu', 'row'))  432 us
    dot_general x4, matrix products, leaf_apply(): jnp.einsum('bcj,bij->bci', pieces, inverse, precision=lax.Precision.HIGHEST)  28.5 us
    dot_general x2, matrix products, shards(): jnp.dot(solved, w_one, precision=highest) * scaling  13.5 us
  transfers between devices with their start and end apart: 3, of which 3 were waited for; matrix products, arithmetic and copies ran while one was open for 1% of the time, Pallas kernels for 0%

commit v1 on v0

v1 whole, which is shorter than its diff:
```python
import functools
import math

import jax
import jax.numpy as jnp
from jax import lax
from jax.experimental import pallas as pl
from jax.experimental.pallas import tpu as pltpu
from jax.sharding import Mesh, PartitionSpec as P


AXES = ("z", "core", "yh", "yl", "x")
SLOT = ("z", "core", "yh")
LOCAL = ("yl", "x")
LEAVES_PER_STEP = 4


def halves(value):
    high = value.astype(jnp.bfloat16)
    low = (value - high.astype(jnp.float32)).astype(jnp.bfloat16)
    return high, low


def main_kernel(held, rhs, linv, w_one, w_two, z_out, high_out, low_out, msg, total):
    step = pl.program_id(0)
    cols = rhs.shape[0]
    leaf = linv.shape[1]
    rank = w_one.shape[1]

    @pl.when(step == 0)
    def _():
        total[...] = jnp.zeros_like(total)

    for j in range(linv.shape[0]):
        span = slice(j * leaf, (j + 1) * leaf)
        a = w_one[span, :]
        e = w_two[span, :]
        x = jnp.concatenate([rhs[:, span], a.T, e.T], axis=0)
        x_high, x_low = halves(x)
        l_high, l_low = halves(linv[j])
        y = lax.dot_general(
            jnp.concatenate([x_high, x_high, x_low], axis=1),
            jnp.concatenate([l_high, l_low, l_high], axis=1),
            (((1,), (1,)), ((), ())),
            preferred_element_type=jnp.float32,
        )
        y_high, y_low = halves(y)
        z_out[:, span] = y[:cols]
        high_out[:, span] = y_high[cols:]
        low_out[:, span] = y_low[cols:]
        w_high, w_low = halves(jnp.concatenate([a, e], axis=1))
        total[...] += jnp.dot(
            jnp.concatenate([y_high, y_high, y_low], axis=1),
            jnp.concatenate([w_high, w_low, w_high], axis=0),
            preferred_element_type=jnp.float32,
        )

    @pl.when(step == pl.num_programs(0) - 1)
    def _():
        slot = (lax.axis_index("z") * 2 + lax.axis_index("core")) * 2 + lax.axis_index("yh")
        position = lax.rem(held[slot], 4)
        parts = msg.shape[0]
        wide = cols // parts
        narrow = rank // parts
        for i in range(parts):
            rows = slice(i * wide, (i + 1) * wide)
            msg[i, :wide, :] = total[rows, :rank]
            msg[i, wide:, :] = total[rows, rank:]

        @pl.when(position == 1)
        def _():
            for i in range(parts):
                rows = slice(cols + i * narrow, cols + (i + 1) * narrow)
                msg[i, :narrow, :] = total[rows, rank:]

        @pl.when(position == 2)
        def _():
            for i in range(parts):
                rows = slice(cols + rank + i * narrow, cols + rank + (i + 1) * narrow)
                msg[i, wide : wide + narrow, :] = total[rows, :rank]


def main_call(rhs, linv, w_one, w_two, held, parts):
    cols, rows = rhs.shape
    leaf = linv.shape[1]
    rank = w_one.shape[1]
    per = LEAVES_PER_STEP
    return pl.pallas_call(
        main_kernel,
        grid_spec=pltpu.PrefetchScalarGridSpec(
            num_scalar_prefetch=1,
            grid=(rows // (leaf * per),),
            in_specs=[
                pl.BlockSpec((cols, leaf * per), lambda i, h: (0, i)),
                pl.BlockSpec((per, leaf, leaf), lambda i, h: (i, 0, 0)),
                pl.BlockSpec((leaf * per, rank), lambda i, h: (i, 0)),
                pl.BlockSpec((leaf * per, rank), lambda i, h: (i, 0)),
            ],
            out_specs=[
                pl.BlockSpec((cols, leaf * per), lambda i, h: (0, i)),
                pl.BlockSpec((2 * rank, leaf * per), lambda i, h: (0, i)),
                pl.BlockSpec((2 * rank, leaf * per), lambda i, h: (0, i)),
                pl.BlockSpec((parts, 2 * cols // parts, rank), lambda i, h: (0, 0, 0)),
            ],
            scratch_shapes=[pltpu.VMEM((cols + 2 * rank, 2 * rank), jnp.float32)],
        ),
        out_shape=[
            jax.ShapeDtypeStruct((cols, rows), jnp.float32),
            jax.ShapeDtypeStruct((2 * rank, rows), jnp.bfloat16),
            jax.ShapeDtypeStruct((2 * rank, rows), jnp.bfloat16),
            jax.ShapeDtypeStruct((parts, 2 * cols // parts, rank), jnp.float32),
        ],
        compiler_params=pltpu.CompilerParams(vmem_limit_bytes=60 * 2**20),
        name="leaves",
    )(held, rhs, linv, w_one, w_two)


def pick_kernel(held, got, out):
    slots = got.shape[0]
    wide = got.shape[1] // 2
    rank = got.shape[2]
    slot = (lax.axis_index("z") * 2 + lax.axis_index("core")) * 2 + lax.axis_index("yh")
    base = (held[slot] // 4) * 4
    place = [jnp.int32(0)] * 3
    for s in range(slots):
        for p in range(3):
            place[p] = jnp.where(held[s] == base + p, s, place[p])
    block_a = got[place[0]]
    block_b = got[place[1]]
    block_c = got[place[2]]
    narrow = (out.shape[1] - 3 * wide) // 2
    pieces = jnp.concatenate(
        [
            block_a[:wide],
            block_a[wide:] + block_b[wide:],
            block_c[:wide],
            block_b[:narrow],
            block_c[wide : wide + narrow],
        ],
        axis=0,
    )
    for i in range(out.shape[0]):
        out[i] = pieces


def pick_call(got, held, parts):
    slots, height, rank = got.shape
    out_height = 3 * height // 2 + 2 * (rank // parts)
    return pl.pallas_call(
        pick_kernel,
        in_specs=[
            pl.BlockSpec(memory_space=pltpu.SMEM),
            pl.BlockSpec(memory_space=pltpu.VMEM),
        ],
        out_specs=pl.BlockSpec(memory_space=pltpu.VMEM),
        out_shape=jax.ShapeDtypeStruct((parts, out_height, rank), jnp.float32),
        name="pick",
    )(held, got)


def last_kernel(scaling, held, ranks, got, z, high, low, out, c_left):
    cols = z.shape[0]
    parts, height, rank = got.shape
    wide = cols // parts
    narrow = rank // parts
    slot = (lax.axis_index("z") * 2 + lax.axis_index("core")) * 2 + lax.axis_index("yh")
    cluster = held[slot]
    position = lax.rem(cluster, 4)
    tree = cluster // 4

    @pl.when(pl.program_id(0) == 0)
    def _():
        def mat(start, size):
            return got[:, start : start + size, :].reshape(parts * size, rank)

        def masked(value, limit):
            lane = lax.broadcasted_iota(jnp.int32, value.shape, 1)
            return jnp.where(lane < limit, value * scaling, 0.0)

        def times(left, right):
            return jnp.dot(
                left, right, precision=lax.Precision.HIGHEST, preferred_element_type=jnp.float32
            )

        one = masked(mat(0, wide), ranks[2 * tree])
        two = mat(wide, wide) - times(one, mat(3 * wide, narrow))
        two = masked(two, ranks[8 + tree])
        three = mat(2 * wide, wide) - times(two, mat(3 * wide + narrow, narrow))
        three = masked(three, ranks[2 * tree + 1])
        left = jnp.where(position == 1, one, jnp.where(position == 3, three, 0.0))
        right = jnp.where(position >= 2, two, 0.0)
        c_high, c_low = halves(jnp.concatenate([left, right], axis=1))
        c_left[...] = jnp.concatenate([c_high, c_high, c_low], axis=1)

    out[...] = z[...] - jnp.dot(
        c_left[...],
        jnp.concatenate([high[...], low[...], high[...]], axis=0),
        preferred_element_type=jnp.float32,
    )


def last_call(got, z, high, low, held, ranks, scaling):
    cols, rows = z.shape
    rank2 = high.shape[0]
    block = 1024
    return pl.pallas_call(
        functools.partial(last_kernel, scaling),
        grid_spec=pltpu.PrefetchScalarGridSpec(
            num_scalar_prefetch=2,
            grid=(rows // block,),
            in_specs=[
                pl.BlockSpec(got.shape, lambda i, h, r: (0, 0, 0)),
                pl.BlockSpec((cols, block), lambda i, h, r: (0, i)),
                pl.BlockSpec((rank2, block), lambda i, h, r: (0, i)),
                pl.BlockSpec((rank2, block), lambda i, h, r: (0, i)),
            ],
            out_specs=pl.BlockSpec((cols, block), lambda i, h, r: (0, i)),
            scratch_shapes=[pltpu.VMEM((cols, 3 * rank2), jnp.bfloat16)],
        ),
        out_shape=jax.ShapeDtypeStruct((cols, rows), jnp.float32),
        compiler_params=pltpu.CompilerParams(vmem_limit_bytes=60 * 2**20),
        name="correct",
    )(held, ranks, got, z, high, low)


def swap(value, axes):
    return lax.all_to_all(value, axes, 0, 0, tiled=True)


def shards(scaling, rhs, linv, w_one, w_two, held, ranks):
    parts = lax.axis_size(LOCAL)
    slots = lax.axis_size(SLOT)
    z, high, low, msg = main_call(rhs, linv, w_one, w_two, held, parts)
    own = jnp.sum(swap(msg, LOCAL), axis=0)
    got = swap(jnp.broadcast_to(own[None], (slots,) + own.shape), SLOT)
    shared = swap(pick_call(got, held, parts), LOCAL)
    return last_call(shared, z, high, low, held, ranks, scaling)


def solution(mesh):
    fine = Mesh(mesh.devices.reshape(4, 2, 2, 2, 4), AXES)
    scaling = 1.0 / math.sqrt(32768)
    in_specs = (P(None, AXES), P(AXES, None, None), P(AXES, None), P(AXES, None), P(), P())
    return jax.shard_map(
        functools.partial(shards, scaling),
        mesh=fine,
        in_specs=in_specs,
        out_specs=P(None, AXES),
        check_vma=False,
    )
```

time: 545 us -> 70.7 us (0.13); the launches traced: 537 us -> 70.3 us
  waiting for transfers between devices: 432 us -> 0 us
  matrix products: 72.5 us -> 0 us
  blocking collectives: 0 us -> 46.6 us
  Pallas kernels: 0 us -> 23.7 us
  between operations: 18.3 us -> 0.02 us
  other arithmetic: 8.26 us -> 0.02 us
  local copies, waits for them, and re-layouts: 5.64 us -> 0.04 us
    psum x3 -> x0, waiting for transfers between devices: 432 us -> none  [couple(): summed_trees = lax.psum(slotted, ('clu', 'row'))]
    dot_general x13 -> x0, matrix products: 72.5 us -> none  [the longest x4 28.5 us: leaf_apply(): jnp.einsum('bcj,bij->bci', pieces, inverse, precision=lax.Precision.HIGHEST)]
    all_to_all x0 -> x3, blocking collectives: none -> 46.6 us  [swap(): return lax.all_to_all(value, axes, 0, 0, tiled=True)]
    pallas_call x0 -> x3, Pallas kernels: none -> 23.7 us  [the longest x1 13.5 us: main_call(): pl.pallas_call(main_kernel, grid_spec=pltpu.PrefetchScalarGridSpec(num_sc...]
    reshape x1 -> x0, local copies, waits for them, and re-layouts: 5.59 us -> none  [leaf_apply(): result.transpose(1, 0, 2).reshape(values.shape[0], blocks * leaf_width)]
  transfers between devices with their start and end apart: 3 -> 0, of which waited for: 3 -> 0; matrix products, arithmetic and copies ran while one was open for 1% -> 0% of each run, Pallas kernels for 0% -> 0%
where the time goes in v1:
time: 70.7 us; the launch traced here: 70.3 us
  blocking collectives  46.6 us (66%)
  Pallas kernels  23.7 us (34%)
    all_to_all x3, blocking collectives, swap(): return lax.all_to_all(value, axes, 0, 0, tiled=True)  46.6 us
    pallas_call x1, Pallas kernels, main_call(): pl.pallas_call(main_kernel, grid_spec=pltpu.PrefetchScalarGridSpec(num_sc...  13.5 us
    pallas_call x1, Pallas kernels, last_call(): pl.pallas_call(functools.partial(last_kernel, scaling), grid_spec=pltpu.P...  8.28 us
    pallas_call x1, Pallas kernels, pick_call(): pl.pallas_call(pick_kernel, in_specs=[pl.BlockSpec(memory_space=pltpu.SME...  1.92 us

profile of v1, /device:TPU:1, one launch (start us, length us, event | category | flops | bytes accessed | tf_op | source)
XLA Modules:
  0.0 70.3 jit_solution(5498009887575197104)
XLA Ops:
  0.0 13.5 %leaves.1 = (f32[256,4096]{1,0:T(8,128)}, bf16[256,4096]{1,0:T(8,128)(2,1)}, bf16[256,4096]{1,0:T(8,128)(2,1)}, f32[8,64,128]{2,1,0:T(8,128)}) custom-call(s32[16]{0:T(128)} %held.5, f32[256,4096]{1,0:T(8,128)} %rhs.1, f32[16,256,256]{2,1,0:T(8,128)} %linv.1, f32[4096,128]{1,0:T(8,128)} %w_one.1, f32[4096,128]{1,0:T(8,128)} %w_two.1), custom_call_target="tpu_custom_call" | custom-call | tf_op jit(solution)/shard_map/leaves/pallas_call | solution.py:88
  13.5 12.2 %all_to_all.15 = f32[8,64,128]{2,1,0:T(8,128)S(1)} all-to-all(f32[8,64,128]{2,1,0:T(8,128)} %get-tuple-element.9), channel_id=1, replica_groups=mesh['z'=4,'core'=2,'yh'=2,'yl'=2,'x'=4] {'yl','x'}, dimensions={0} | all-to-all | bytes 524288 | tf_op jit(solution)/shard_map/all_to_all | solution.py:227
  25.7 19.9 %all_to_all.16.got = f32[16,64,128]{2,1,0:T(8,128)} all-to-all(f32[16,64,128]{2,1,0:T(8,128)S(1)} %broadcast_in_dim.2), channel_id=1, replica_groups=mesh['z'=4,'core'=2,'yh'=2,'yl'=2,'x'=4] {'z','core','yh'}, dimensions={0} | all-to-all | bytes 1048576 | tf_op jit(solution)/shard_map/all_to_all | solution.py:227
  45.6 1.9 %pick.1 = f32[8,128,128]{2,1,0:T(8,128)} custom-call(s32[16]{0:T(128)} %held.5, f32[16,64,128]{2,1,0:T(8,128)} %all_to_all.16.got), custom_call_target="tpu_custom_call" | custom-call | tf_op jit(solution)/shard_map/pick/pallas_call | solution.py:149
  47.6 14.5 %all_to_all.17.got = f32[8,128,128]{2,1,0:T(8,128)} all-to-all(f32[8,128,128]{2,1,0:T(8,128)} %pick.1), channel_id=1, replica_groups=mesh['z'=4,'core'=2,'yh'=2,'yl'=2,'x'=4] {'yl','x'}, dimensions={0} | all-to-all | bytes 1048576 | tf_op jit(solution)/shard_map/all_to_all | solution.py:227
  62.0 8.3 %correct.1 = f32[256,4096]{1,0:T(8,128)} custom-call(s32[16]{0:T(128)} %held.5, s32[12]{0:T(128)} %ranks.1, f32[8,128,128]{2,1,0:T(8,128)} %all_to_all.17.got, f32[256,4096]{1,0:T(8,128)} %get-tuple-element.10.z, bf16[256,4096]{1,0:T(8,128)(2,1)} %get-tuple-element.11.high, bf16[256,4096]{1,0:T(8,128)(2,1)} %get-tuple-element.12.low), custom_call_target="tpu_custom_call" | custom-call | tf_op jit(solution)/shard_map/correct/pallas_call | solution.py:206
  (2 shorter events, 0.1 us)

commit v2 on v0

v2 whole, which is shorter than its diff:
```python
import functools
import math

import jax
import jax.numpy as jnp
from jax import lax
from jax.experimental import pallas as pl
from jax.experimental.pallas import tpu as pltpu
from jax.sharding import Mesh, PartitionSpec as P


AXES = ("z", "core", "yh", "yl", "x")
SLOT = ("z", "yh")
LOCAL = ("yl", "x")
GROUP = 2
CHUNK = 512


def halves(value):
    high = value.astype(jnp.bfloat16)
    low = (value - high.astype(jnp.float32)).astype(jnp.bfloat16)
    return high, low


def split3(value):
    high, low = halves(value)
    return jnp.concatenate([high, high, low], axis=1)


def nt(left, right):
    return lax.dot_general(
        left, right, (((1,), (1,)), ((), ())), preferred_element_type=jnp.float32
    )


def own_slot():
    return (lax.axis_index("z") * 2 + lax.axis_index("core")) * 2 + lax.axis_index("yh")


def main_kernel(
    held_in, rhs, linv, w_one, w_two, z, high, low, msg,
    held, rhs_v, linv_v, w_v, total, even, odd, held_sem, sems,
):
    cols = rhs.shape[0]
    leaves, leaf, _ = linv.shape
    rank = w_one.shape[1]
    groups = leaves // GROUP
    parts = msg.shape[0]
    wide = cols // parts
    narrow = rank // parts

    def copies(g):
        rows = pl.ds(g * (GROUP * leaf), GROUP * leaf)
        pair = pl.ds(g * GROUP, GROUP)
        return [
            pltpu.make_async_copy(rhs.at[:, rows], rhs_v.at[:, rows], sems.at[0, g]),
            pltpu.make_async_copy(linv.at[pair], linv_v.at[pair], sems.at[1, g]),
            pltpu.make_async_copy(w_one.at[rows], w_v.at[0, rows], sems.at[2, g]),
            pltpu.make_async_copy(w_two.at[rows], w_v.at[1, rows], sems.at[3, g]),
        ]

    held_copy = pltpu.make_async_copy(held_in, held, held_sem)
    held_copy.start()
    for g in range(groups):
        for copy in copies(g):
            copy.start()
    msg[...] = jnp.zeros_like(msg)
    held_copy.wait()
    position = lax.rem(held[own_slot()], 4)

    def span_of(i):
        return pl.ds(pl.multiple_of(i * leaf, leaf), leaf)

    def wait(g):
        for copy in copies(g):
            copy.wait()

    def each_leaf(solve, couple):
        wait(0)
        solve(0, even)

        def pair(k, carry):
            wait(k + 1)
            couple(2 * k, even)
            solve(2 * k + 1, odd)
            couple(2 * k + 1, odd)
            solve(2 * k + 2, even)
            return carry

        lax.fori_loop(0, groups - 1, pair, 0)
        couple(leaves - 2, even)
        solve(leaves - 1, odd)
        couple(leaves - 1, odd)

    def leaf_product(x, i):
        l_high, l_low = halves(linv_v[i])
        return nt(split3(x), jnp.concatenate([l_high, l_low, l_high], axis=1))

    @pl.when(position == 0)
    def _():
        total[:cols] = jnp.zeros((cols, 2 * rank), jnp.float32)

        def solve(i, kept):
            span = span_of(i)
            y = leaf_product(rhs_v[:, span], i)
            z[:, span] = y
            y_high, y_low = halves(y)
            kept[0, :cols] = y_high
            kept[1, :cols] = y_low

        def couple(i, kept):
            span = span_of(i)
            w = jnp.concatenate([w_v[0, span, :], w_v[1, span, :]], axis=1)
            w_high, w_low = halves(w)
            y_high = kept[0, :cols]
            total[:cols] += jnp.dot(
                jnp.concatenate([y_high, y_high, kept[1, :cols]], axis=1),
                jnp.concatenate([w_high, w_low, w_high], axis=0),
                preferred_element_type=jnp.float32,
            )

        each_leaf(solve, couple)
        for i in range(parts):
            rows = slice(i * wide, (i + 1) * wide)
            msg[i, :wide, :] = total[rows, :rank]
            msg[i, wide:, :] = total[rows, rank:]

    @pl.when((position == 1) | (position == 2))
    def _():
        mine = position - 1
        other = 2 - position
        total[...] = jnp.zeros_like(total)

        def solve(i, kept):
            span = span_of(i)
            x = jnp.concatenate([rhs_v[:, span], w_v[mine, span, :].T], axis=0)
            y = leaf_product(x, i)
            y_high, y_low = halves(y)
            z[:, span] = y[:cols]
            high[:rank, span] = y_high[cols:]
            low[:rank, span] = y_low[cols:]
            kept[0] = y_high
            kept[1] = y_low

        def couple(i, kept):
            w_high, w_low = halves(w_v[other, span_of(i), :])
            right = jnp.concatenate([w_high, w_low], axis=1)
            total[...] += jnp.dot(
                jnp.concatenate([kept[0], kept[1]], axis=1),
                jnp.concatenate([right, right], axis=0),
                preferred_element_type=jnp.float32,
            )

        each_leaf(solve, couple)
        total[:, :rank] = total[:, :rank] + total[:, rank:]
        for i in range(parts):
            rows = slice(i * wide, (i + 1) * wide)
            cross = slice(cols + i * narrow, cols + (i + 1) * narrow)

            @pl.when(position == 1)
            def _():
                msg[i, :narrow, :] = total[cross, :rank]
                msg[i, wide:, :] = total[rows, :rank]

            @pl.when(position == 2)
            def _():
                msg[i, :wide, :] = total[rows, :rank]
                msg[i, wide : wide + narrow, :] = total[cross, :rank]

    @pl.when(position == 3)
    def _():
        def solve(i, kept):
            span = span_of(i)
            x = jnp.concatenate(
                [rhs_v[:, span], w_v[0, span, :].T, w_v[1, span, :].T], axis=0
            )
            y = leaf_product(x, i)
            y_high, y_low = halves(y[cols:])
            z[:, span] = y[:cols]
            high[:, span] = y_high
            low[:, span] = y_low

        each_leaf(solve, lambda i, kept: None)


def main_call(rhs, linv, w_one, w_two, held, parts):
    cols, rows = rhs.shape
    leaves, leaf, _ = linv.shape
    rank = w_one.shape[1]
    arrays = [
        pltpu.with_memory_space_constraint(v, pltpu.HBM)
        for v in (held, rhs, linv, w_one, w_two)
    ]
    return pl.pallas_call(
        main_kernel,
        in_specs=[pl.BlockSpec(memory_space=pltpu.HBM)] * 5,
        out_specs=[pl.BlockSpec(memory_space=pltpu.VMEM)] * 4,
        out_shape=[
            pltpu.VMEM((cols, rows), jnp.float32),
            pltpu.VMEM((2 * rank, rows), jnp.bfloat16),
            pltpu.VMEM((2 * rank, rows), jnp.bfloat16),
            pltpu.VMEM((parts, 2 * cols // parts, rank), jnp.float32),
        ],
        scratch_shapes=[
            pltpu.SMEM(held.shape, jnp.int32),
            pltpu.VMEM((cols, rows), jnp.float32),
            pltpu.VMEM((leaves, leaf, leaf), jnp.float32),
            pltpu.VMEM((2, rows, rank), jnp.float32),
            pltpu.VMEM((cols + rank, 2 * rank), jnp.float32),
            pltpu.VMEM((2, cols + rank, leaf), jnp.bfloat16),
            pltpu.VMEM((2, cols + rank, leaf), jnp.bfloat16),
            pltpu.SemaphoreType.DMA(()),
            pltpu.SemaphoreType.DMA((4, leaves // GROUP)),
        ],
        compiler_params=pltpu.CompilerParams(vmem_limit_bytes=40 * 2**20),
        name="leaves",
    )(*arrays)


def fold_kernel(got, out):
    value = got[0]
    for i in range(1, got.shape[0]):
        value = value + got[i]
    for i in range(out.shape[0]):
        out[i] = value


def fold_call(got, count):
    return pl.pallas_call(
        fold_kernel,
        in_specs=[pl.BlockSpec(memory_space=pltpu.VMEM)],
        out_specs=pl.BlockSpec(memory_space=pltpu.VMEM),
        out_shape=pltpu.VMEM((count,) + got.shape[1:], jnp.float32),
        compiler_params=pltpu.CompilerParams(vmem_limit_bytes=4 * 2**20),
        name="fold",
    )(pltpu.with_memory_space_constraint(got, pltpu.VMEM))


def pick_kernel(held, got, own, other):
    height, rank = own.shape
    wide = got.shape[1] // 2
    narrow = (height - 3 * wide) // 2
    core = lax.axis_index("core")
    for out, where in ((own, core), (other, 1 - core)):
        slot = (lax.axis_index("z") * 2 + where) * 2 + lax.axis_index("yh")
        base = (held[slot] // 4) * 4
        blocks = []
        for p in range(3):
            place = jnp.int32(0)
            here = jnp.int32(0)
            for s in range(2 * got.shape[0]):
                hit = held[s] == base + p
                place = jnp.where(hit, (s // 4) * 2 + s % 2, place)
                here = jnp.where(hit & (core == (s // 2) % 2), 1, here)
            blocks.append(jnp.where(here == 1, got[place], 0.0))
        a, b, c = blocks
        out[:wide] = a[:wide]
        out[wide : 2 * wide] = a[wide:] + b[wide:]
        out[2 * wide : 3 * wide] = c[:wide]
        out[3 * wide : 3 * wide + narrow] = b[:narrow]
        out[3 * wide + narrow :] = c[wide : wide + narrow]


def pick_call(got, held, parts):
    slots, height, rank = got.shape
    out_height = 3 * height // 2 + 2 * (rank // parts)
    return pl.pallas_call(
        pick_kernel,
        in_specs=[
            pl.BlockSpec(memory_space=pltpu.SMEM),
            pl.BlockSpec(memory_space=pltpu.VMEM),
        ],
        out_specs=[pl.BlockSpec(memory_space=pltpu.VMEM)] * 2,
        out_shape=[pltpu.VMEM((out_height, rank), jnp.float32)] * 2,
        compiler_params=pltpu.CompilerParams(vmem_limit_bytes=4 * 2**20),
        name="pick",
    )(held, pltpu.with_memory_space_constraint(got, pltpu.VMEM))


def last_kernel(scaling, held, ranks, got, z, high, low, out, solved, sems):
    cols, rows = z.shape
    parts, height, rank = got.shape
    wide = cols // parts
    narrow = rank // parts
    cluster = held[own_slot()]
    position = lax.rem(cluster, 4)
    tree = cluster // 4
    count = rows // CHUNK

    def mat(start, size):
        return got[:, start : start + size, :].reshape(parts * size, rank)

    def masked(value, limit):
        lane = lax.broadcasted_iota(jnp.int32, value.shape, 1)
        return jnp.where(lane < limit, value * scaling, 0.0)

    def times(left, right):
        return jnp.dot(
            left, right, precision=lax.Precision.HIGHEST, preferred_element_type=jnp.float32
        )

    def first():
        return masked(mat(0, wide), ranks[2 * tree])

    def second():
        value = mat(wide, wide) - times(first(), mat(3 * wide, narrow))
        return masked(value, ranks[8 + tree])

    def send(source, i):
        span = pl.ds(i * CHUNK, CHUNK)
        return pltpu.make_async_copy(source.at[:, span], out.at[:, span], sems.at[i])

    def correct(coef):
        depth = coef.shape[1]
        left = split3(coef)
        for i in range(count):
            span = slice(i * CHUNK, (i + 1) * CHUNK)
            h = high[:depth, span]
            solved[:, span] = z[:, span] - jnp.dot(
                left,
                jnp.concatenate([h, low[:depth, span], h], axis=0),
                preferred_element_type=jnp.float32,
            )
            send(solved, i).start()
        for i in range(count):
            send(solved, i).wait()

    @pl.when(position == 0)
    def _():
        for i in range(count):
            send(z, i).start()
        for i in range(count):
            send(z, i).wait()

    @pl.when(position == 1)
    def _():
        correct(first())

    @pl.when(position == 2)
    def _():
        correct(second())

    @pl.when(position == 3)
    def _():
        two = second()
        value = mat(2 * wide, wide) - times(two, mat(3 * wide + narrow, narrow))
        correct(jnp.concatenate([masked(value, ranks[2 * tree + 1]), two], axis=1))


def last_call(got, z, high, low, held, ranks, scaling):
    cols, rows = z.shape
    arrays = [pltpu.with_memory_space_constraint(v, pltpu.VMEM) for v in (got, z, high, low)]
    return pl.pallas_call(
        functools.partial(last_kernel, scaling),
        in_specs=[pl.BlockSpec(memory_space=pltpu.SMEM)] * 2
        + [pl.BlockSpec(memory_space=pltpu.VMEM)] * 4,
        out_specs=pl.BlockSpec(memory_space=pltpu.HBM),
        out_shape=pltpu.HBM((cols, rows), jnp.float32),
        scratch_shapes=[
            pltpu.VMEM((cols, rows), jnp.float32),
            pltpu.SemaphoreType.DMA((rows // CHUNK,)),
        ],
        compiler_params=pltpu.CompilerParams(vmem_limit_bytes=16 * 2**20),
        name="correct",
    )(held, ranks, *arrays)


def swap(value, axes):
    return lax.all_to_all(value, axes, 0, 0, tiled=True)


def copied(value, count):
    return jnp.broadcast_to(value[None], (count,) + value.shape)


def shards(scaling, rhs, linv, w_one, w_two, held, ranks):
    parts = lax.axis_size(LOCAL)
    z, high, low, msg = main_call(rhs, linv, w_one, w_two, held, parts)
    got = swap(fold_call(swap(msg, LOCAL), lax.axis_size(SLOT)), SLOT)
    mine, other = pick_call(got, held, parts)
    mine = mine + lax.ppermute(other, "core", [(0, 1), (1, 0)])
    shared = swap(copied(mine, parts), LOCAL)
    return last_call(shared, z, high, low, held, ranks, scaling)


def solution(mesh):
    fine = Mesh(mesh.devices.reshape(4, 2, 2, 2, 4), AXES)
    scaling = 1.0 / math.sqrt(32768)
    in_specs = (P(None, AXES), P(AXES, None, None), P(AXES, None), P(AXES, None), P(), P())
    return jax.shard_map(
        functools.partial(shards, scaling),
        mesh=fine,
        in_specs=in_specs,
        out_specs=P(None, AXES),
        check_vma=False,
    )
```

time: 545 us -> 56.1 us (0.10); the launches traced: 537 us -> 55.8 us
  waiting for transfers between devices: 432 us -> 0.9 us
  matrix products: 72.5 us -> 0 us
  blocking collectives: 0 us -> 38.9 us
  between operations: 18.3 us -> 0.04 us
  Pallas kernels: 0 us -> 12.1 us
  other arithmetic: 8.26 us -> 0.01 us
  local copies, waits for them, and re-layouts: 5.64 us -> 0.04 us
    psum x3 -> x0, waiting for transfers between devices: 432 us -> none  [couple(): summed_trees = lax.psum(slotted, ('clu', 'row'))]
    dot_general x13 -> x0, matrix products: 72.5 us -> none  [the longest x4 28.5 us: leaf_apply(): jnp.einsum('bcj,bij->bci', pieces, inverse, precision=lax.Precision.HIGHEST)]
    all_to_all x0 -> x3, blocking collectives: none -> 38.9 us  [swap(): return lax.all_to_all(value, axes, 0, 0, tiled=True)]
    pallas_call x0 -> x4, Pallas kernels: none -> 12.1 us  [the longest x1 8.05 us: main_call(): pl.pallas_call(main_kernel, in_specs=[pl.BlockSpec(memory_space=pltpu.HBM...]
    reshape x1 -> x0, local copies, waits for them, and re-layouts: 5.59 us -> none  [leaf_apply(): result.transpose(1, 0, 2).reshape(values.shape[0], blocks * leaf_width)]
  transfers between devices with their start and end apart: 3 -> 1, of which waited for: 3 -> 1; matrix products, arithmetic and copies ran while one was open for 1% -> 0% of each run, Pallas kernels for 0% -> 0%
where the time goes in v2:
time: 56.1 us; the launch traced here: 55.8 us
  blocking collectives  38.9 us (69%)
  Pallas kernels  12.1 us (22%)
  starting transfers between devices  3.85 us (7%)
  waiting for transfers between devices  0.9 us (2%)
    all_to_all x3, blocking collectives, swap(): return lax.all_to_all(value, axes, 0, 0, tiled=True)  38.9 us
    pallas_call x1, Pallas kernels, main_call(): pl.pallas_call(main_kernel, in_specs=[pl.BlockSpec(memory_space=pltpu.HBM...  8.05 us
    ppermute x1, starting transfers between devices, shards(): mine = mine + lax.ppermute(other, 'core', [(0, 1), (1, 0)])  3.85 us
    pallas_call x1, Pallas kernels, last_call(): pl.pallas_call(functools.partial(last_kernel, scaling), in_specs=[pl.Bloc...  3.34 us
  transfers between devices with their start and end apart: 1, of which 1 were waited for; matrix products, arithmetic and copies ran while one was open for 0% of the time, Pallas kernels for 0%

profile of v2, /device:TPU:1, one launch (start us, length us, event | category | flops | bytes accessed | tf_op | source)
XLA Modules:
  0.0 55.8 jit_solution(17437574680124820569)
XLA Ops:
  0.0 0.0 copy-start
  0.0 0.0 copy-start.1
  0.0 8.1 %leaves.1 = (f32[256,4096]{1,0:T(8,128)S(1)}, bf16[256,4096]{1,0:T(8,128)(2,1)S(1)}, bf16[256,4096]{1,0:T(8,128)(2,1)S(1)}, f32[8,64,128]{2,1,0:T(8,128)S(1)}) custom-call(s32[16]{0:T(128)} %held.3, f32[256,4096]{1,0:T(8,128)} %rhs.1, f32[16,256,256]{2,1,0:T(8,128)} %linv.1, f32[4096,128]{1,0:T(8,128)} %w_one.1, f32[4096,128]{1,0:T(8,128)} %w_two.1), custom_call_target="tpu_custom_call" | custom-call | tf_op jit(solution)/shard_map/leaves/pallas_call | solution.py:194
  8.1 12.0 %all_to_all.15.got = f32[8,64,128]{2,1,0:T(8,128)S(1)} all-to-all(f32[8,64,128]{2,1,0:T(8,128)S(1)} %get-tuple-element.11), channel_id=1, replica_groups=mesh['z'=4,'core'=2,'yh'=2,'yl'=2,'x'=4] {'yl','x'}, dimensions={0} | all-to-all | bytes 524288 | tf_op jit(solution)/shard_map/all_to_all | solution.py:369
  20.0 14.3 %all_to_all.16.got = f32[8,64,128]{2,1,0:T(8,128)S(1)} all-to-all(f32[8,64,128]{2,1,0:T(8,128)S(1)} %fold.1), channel_id=1, replica_groups=mesh['z'=4,'core'=2,'yh'=2,'yl'=2,'x'=4] {'z','yh'}, dimensions={0} | all-to-all | bytes 524288 | tf_op jit(solution)/shard_map/all_to_all | solution.py:369
  34.3 0.0 copy-done
  34.3 0.7 %pick.1 = (f32[128,128]{1,0:T(8,128)S(1)}, f32[128,128]{1,0:T(8,128)S(1)}) custom-call(s32[16]{0:T(128)S(1)} %copy-done, f32[8,64,128]{2,1,0:T(8,128)S(1)} %all_to_all.16.got), custom_call_target="tpu_custom_call" | custom-call | tf_op jit(solution)/shard_map/pick/pallas_call | solution.py:267
  35.0 3.8 %collective-permute-start = (f32[128,128]{1,0:T(8,128)S(1)}, f32[128,128]{1,0:T(8,128)S(1)}, u32[]{:S(2)}, u32[]{:S(2)}) collective-permute-start(f32[128,128]{1,0:T(8,128)S(1)} %get-tuple-element.13), channel_id=1, source_target_pairs={{0,16},{16,0},{1,17},{17,1},{2,18},{18,2},{3,19},{19,3},{4,20},{20... | collective-permute-start | bytes 196616 | tf_op jit(solution)/shard_map/ppermute | solution.py:381
  38.9 0.9 %collective-permute-done = f32[128,128]{1,0:T(8,128)S(1)} collective-permute-done((f32[128,128]{1,0:T(8,128)S(1)}, f32[128,128]{1,0:T(8,128)S(1)}, u32[]{:S(2)}, u32[]{:S(2)}) %collective-permute-start) | collective-permute-done | bytes 65568 | tf_op jit(solution)/shard_map/ppermute | solution.py:381
  39.8 12.6 %all_to_all.17.got = f32[8,128,128]{2,1,0:T(8,128)S(1)} all-to-all(f32[8,128,128]{2,1,0:T(8,128)S(1)} %broadcast_in_dim.2), channel_id=1, replica_groups=mesh['z'=4,'core'=2,'yh'=2,'yl'=2,'x'=4] {'yl','x'}, dimensions={0} | all-to-all | bytes 1048576 | tf_op jit(solution)/shard_map/all_to_all | solution.py:369
  52.5 0.0 copy-done.1
  52.5 3.3 %correct.1 = f32[256,4096]{1,0:T(8,128)} custom-call(s32[16]{0:T(128)S(1)} %copy-done, s32[12]{0:T(128)S(1)} %copy-done.1, f32[8,128,128]{2,1,0:T(8,128)S(1)} %all_to_all.17.got, f32[256,4096]{1,0:T(8,128)S(1)} %get-tuple-element.14.z, bf16[256,4096]{1,0:T(8,128)(2,1)S(1)} %get-tuple-element.15.high, bf16[256,4096]{1,0:T(8,128)(2,1)S(1)} %get-tuple-element.16.low), custom_call_target="tpu_custom_call" | custom-call | tf_op jit(solution)/shard_map/correct/pallas_call | solution.py:353
  (3 shorter events, 0.1 us)
Async XLA Ops:
  0.0 34.3 %copy-start = (s32[16]{0:T(128)S(1)}, s32[16]{0:T(128)}, u32[]{:S(2)}) copy-start(s32[16]{0:T(128)} %held.3) | copy-start | bytes 196
  0.0 52.5 %copy-start.1 = (s32[12]{0:T(128)S(1)}, s32[12]{0:T(128)}, u32[]{:S(2)}) copy-start(s32[12]{0:T(128)} %ranks.1) | copy-start | bytes 148
  35.0 4.7 %collective-permute-start = (f32[128,128]{1,0:T(8,128)S(1)}, f32[128,128]{1,0:T(8,128)S(1)}, u32[]{:S(2)}, u32[]{:S(2)}) collective-permute-start(f32[128,128]{1,0:T(8,128)S(1)} %get-tuple-element.13), channel_id=1, source_target_pairs={{0,16},{16,0},{1,17},{17,1},{2,18},{18,2},{3,19},{19,3},{4,20},{20... | collective-permute-start | bytes 196616 | tf_op jit(solution)/shard_map/ppermute | solution.py:381

commit v3 on v2

v3 whole, which is shorter than its diff:
```python
import functools
import math

import jax
import jax.numpy as jnp
from jax import lax
from jax.experimental import pallas as pl
from jax.experimental.pallas import tpu as pltpu
from jax.sharding import PartitionSpec as P


AXES = ("clu", "row")
GROUP = 2
CHUNK = 512
PER_BLOCK = 8
TILE = 8


def halves(value):
    high = value.astype(jnp.bfloat16)
    low = (value - high.astype(jnp.float32)).astype(jnp.bfloat16)
    return high, low


def split3(value):
    high, low = halves(value)
    return jnp.concatenate([high, high, low], axis=1)


def nt(left, right):
    return lax.dot_general(
        left, right, (((1,), (1,)), ((), ())), preferred_element_type=jnp.float32
    )


def own_slot():
    device = lax.axis_index("clu") * lax.axis_size("row") + lax.axis_index("row")
    return device // PER_BLOCK


def main_kernel(
    held_in, rhs, linv, w_one, w_two, z, lw, msg,
    held, rhs_v, linv_v, w_v, total, even, odd, held_sem, sems,
):
    cols = rhs.shape[0]
    leaves, leaf, _ = linv.shape
    rank = w_one.shape[1]
    groups = leaves // GROUP
    half = cols // 2

    def put(j, block):
        msg[pl.ds(j, half, stride=4), :] = block

    def copies(g):
        rows = pl.ds(g * (GROUP * leaf), GROUP * leaf)
        pair = pl.ds(g * GROUP, GROUP)
        return [
            pltpu.make_async_copy(rhs.at[:, rows], rhs_v.at[:, rows], sems.at[0, g]),
            pltpu.make_async_copy(linv.at[pair], linv_v.at[pair], sems.at[1, g]),
            pltpu.make_async_copy(w_one.at[rows], w_v.at[0, rows], sems.at[2, g]),
            pltpu.make_async_copy(w_two.at[rows], w_v.at[1, rows], sems.at[3, g]),
        ]

    held_copy = pltpu.make_async_copy(held_in, held, held_sem)
    held_copy.start()
    for g in range(groups):
        for copy in copies(g):
            copy.start()
    msg[...] = jnp.zeros_like(msg)
    held_copy.wait()
    position = lax.rem(held[own_slot()], 4)

    def span_of(i):
        return pl.ds(pl.multiple_of(i * leaf, leaf), leaf)

    def wait(g):
        for copy in copies(g):
            copy.wait()

    def each_leaf(solve, couple):
        wait(0)
        solve(0, even)

        def pair(k, carry):
            wait(k + 1)
            couple(2 * k, even)
            solve(2 * k + 1, odd)
            couple(2 * k + 1, odd)
            solve(2 * k + 2, even)
            return carry

        lax.fori_loop(0, groups - 1, pair, 0)
        couple(leaves - 2, even)
        solve(leaves - 1, odd)
        couple(leaves - 1, odd)

    def leaf_product(x, i):
        l_high, l_low = halves(linv_v[i])
        return nt(split3(x), jnp.concatenate([l_high, l_low, l_high], axis=1))

    @pl.when(position == 0)
    def _():
        total[:cols] = jnp.zeros((cols, 2 * rank), jnp.float32)

        def solve(i, kept):
            span = span_of(i)
            y = leaf_product(rhs_v[:, span], i)
            z[:, span] = y
            kept[:cols] = y

        def couple(i, kept):
            span = span_of(i)
            w = jnp.concatenate([w_v[0, span, :], w_v[1, span, :]], axis=1)
            w_high, w_low = halves(w)
            total[:cols] += jnp.dot(
                split3(kept[:cols]),
                jnp.concatenate([w_high, w_low, w_high], axis=0),
                preferred_element_type=jnp.float32,
            )

        each_leaf(solve, couple)
        put(0, total[:half, :rank])
        put(1, total[half:cols, :rank])
        put(2, total[:half, rank:])
        put(3, total[half:cols, rank:])

    @pl.when((position == 1) | (position == 2))
    def _():
        mine = position - 1
        other = 2 - position
        total[...] = jnp.zeros_like(total)

        def solve(i, kept):
            span = span_of(i)
            x = jnp.concatenate([rhs_v[:, span], w_v[mine, span, :].T], axis=0)
            y = leaf_product(x, i)
            z[:, span] = y[:cols]
            lw[:rank, span] = y[cols:]
            kept[...] = y

        def couple(i, kept):
            w_high, w_low = halves(w_v[other, span_of(i), :])
            right = jnp.concatenate([w_high, w_low], axis=1)
            total[...] += jnp.dot(
                jnp.concatenate(halves(kept[...]), axis=1),
                jnp.concatenate([right, right], axis=0),
                preferred_element_type=jnp.float32,
            )

        each_leaf(solve, couple)
        summed = total[:, :rank] + total[:, rank:]

        @pl.when(position == 1)
        def _():
            put(0, summed[cols:])
            put(2, summed[:half])
            put(3, summed[half:cols])

        @pl.when(position == 2)
        def _():
            put(0, summed[:half])
            put(1, summed[half:cols])
            put(2, summed[cols:])

    @pl.when(position == 3)
    def _():
        def solve(i, kept):
            span = span_of(i)
            x = jnp.concatenate(
                [rhs_v[:, span], w_v[0, span, :].T, w_v[1, span, :].T], axis=0
            )
            y = leaf_product(x, i)
            z[:, span] = y[:cols]
            lw[:, span] = y[cols:]

        each_leaf(solve, lambda i, kept: None)


def main_call(rhs, linv, w_one, w_two, held):
    cols, rows = rhs.shape
    leaves, leaf, _ = linv.shape
    rank = w_one.shape[1]
    arrays = [
        pltpu.with_memory_space_constraint(v, pltpu.HBM)
        for v in (held, rhs, linv, w_one, w_two)
    ]
    return pl.pallas_call(
        main_kernel,
        in_specs=[pl.BlockSpec(memory_space=pltpu.HBM)] * 5,
        out_specs=[pl.BlockSpec(memory_space=pltpu.VMEM)] * 3,
        out_shape=[
            pltpu.VMEM((cols, rows), jnp.float32),
            pltpu.VMEM((2 * rank, rows), jnp.float32),
            pltpu.VMEM((2 * cols, rank), jnp.float32),
        ],
        scratch_shapes=[
            pltpu.SMEM(held.shape, jnp.int32),
            pltpu.VMEM((cols, rows), jnp.float32),
            pltpu.VMEM((leaves, leaf, leaf), jnp.float32),
            pltpu.VMEM((2, rows, rank), jnp.float32),
            pltpu.VMEM((cols + rank, 2 * rank), jnp.float32),
            pltpu.VMEM((cols + rank, leaf), jnp.float32),
            pltpu.VMEM((cols + rank, leaf), jnp.float32),
            pltpu.SemaphoreType.DMA(()),
            pltpu.SemaphoreType.DMA((4, leaves // GROUP)),
        ],
        compiler_params=pltpu.CompilerParams(vmem_limit_bytes=40 * 2**20),
        name="leaves",
    )(*arrays)


def pick_kernel(held, got, out, place, sums, trees):
    slots = held.shape[0]
    block = got.shape[0] // slots
    for s in range(slots):
        place[held[s]] = s
        value = got[s * block : s * block + TILE]
        for i in range(1, block // TILE):
            value = value + got[s * block + i * TILE : s * block + (i + 1) * TILE]
        value = value + pltpu.roll(value, TILE // 2, 0)
        sums[s * TILE : (s + 1) * TILE] = value
    row = lax.broadcasted_iota(jnp.int32, (TILE, got.shape[1]), 0)
    for t in range(slots // 4):

        def block_of(p):
            return sums[pl.ds(pl.multiple_of(place[4 * t + p] * TILE, TILE), TILE), :]

        a, b, c = block_of(0), block_of(1), block_of(2)
        tail = jnp.where(row == 6, pltpu.roll(b, 2, 0), pltpu.roll(c, 1, 0))
        tile = jnp.where(row < 2, a, jnp.where(row < 4, a + b, jnp.where(row < 6, c, tail)))
        trees[t * TILE : (t + 1) * TILE] = tile
    for s in range(slots):
        tile = trees[pl.ds(pl.multiple_of(held[s] // 4 * TILE, TILE), TILE), :]
        for i in range(PER_BLOCK):
            out[(s * PER_BLOCK + i) * TILE : (s * PER_BLOCK + i + 1) * TILE] = tile


def pick_call(got, held):
    rows, rank = got.shape
    slots = held.shape[0]
    return pl.pallas_call(
        pick_kernel,
        in_specs=[
            pl.BlockSpec(memory_space=pltpu.SMEM),
            pl.BlockSpec(memory_space=pltpu.VMEM),
        ],
        out_specs=pl.BlockSpec(memory_space=pltpu.VMEM),
        out_shape=pltpu.VMEM((slots * PER_BLOCK * TILE, rank), jnp.float32),
        scratch_shapes=[
            pltpu.SMEM((slots,), jnp.int32),
            pltpu.VMEM((slots * TILE, rank), jnp.float32),
            pltpu.VMEM((slots // 4 * TILE, rank), jnp.float32),
        ],
        compiler_params=pltpu.CompilerParams(vmem_limit_bytes=4 * 2**20),
        name="pick",
    )(held, pltpu.with_memory_space_constraint(got, pltpu.VMEM))


def last_kernel(scaling, held, ranks, got, z, lw, out, solved, sems):
    cols, rows = z.shape
    devices = got.shape[0] // TILE
    rank = got.shape[1]
    cluster = held[own_slot()]
    position = lax.rem(cluster, 4)
    tree = cluster // 4
    count = rows // CHUNK

    def mat(*rows):
        pieces = [got[pl.ds(j, devices, stride=TILE), :] for j in rows]
        return jnp.concatenate(pieces, axis=0)

    def masked(value, limit):
        lane = lax.broadcasted_iota(jnp.int32, value.shape, 1)
        return jnp.where(lane < limit, value * scaling, 0.0)

    def times(left, right):
        r_high, r_low = halves(right)
        return jnp.dot(
            left,
            jnp.concatenate([r_high, r_low, r_high], axis=0),
            preferred_element_type=jnp.float32,
        )

    def first():
        return masked(mat(0, 1), ranks[2 * tree])

    def second():
        value = mat(2, 3) - times(split3(first()), mat(6))
        return masked(value, ranks[8 + tree])

    def send(source, i):
        span = pl.ds(i * CHUNK, CHUNK)
        return pltpu.make_async_copy(source.at[:, span], out.at[:, span], sems.at[i])

    def correct(coef):
        depth = coef.shape[1]
        left = split3(coef)
        for i in range(count):
            span = slice(i * CHUNK, (i + 1) * CHUNK)
            solved[:, span] = z[:, span] - times(left, lw[:depth, span])
            send(solved, i).start()
        for i in range(count):
            send(solved, i).wait()

    @pl.when(position == 0)
    def _():
        for i in range(count):
            send(z, i).start()
        for i in range(count):
            send(z, i).wait()

    @pl.when(position == 1)
    def _():
        correct(first())

    @pl.when(position == 2)
    def _():
        correct(second())

    @pl.when(position == 3)
    def _():
        two = second()
        value = mat(4, 5) - times(split3(two), mat(7))
        correct(jnp.concatenate([masked(value, ranks[2 * tree + 1]), two], axis=1))


def last_call(got, z, lw, held, ranks, scaling):
    cols, rows = z.shape
    arrays = [pltpu.with_memory_space_constraint(v, pltpu.VMEM) for v in (got, z, lw)]
    return pl.pallas_call(
        functools.partial(last_kernel, scaling),
        in_specs=[pl.BlockSpec(memory_space=pltpu.SMEM)] * 2
        + [pl.BlockSpec(memory_space=pltpu.VMEM)] * 3,
        out_specs=pl.BlockSpec(memory_space=pltpu.HBM),
        out_shape=pltpu.HBM((cols, rows), jnp.float32),
        scratch_shapes=[
            pltpu.VMEM((cols, rows), jnp.float32),
            pltpu.SemaphoreType.DMA((rows // CHUNK,)),
        ],
        compiler_params=pltpu.CompilerParams(vmem_limit_bytes=16 * 2**20),
        name="correct",
    )(held, ranks, *arrays)


def swap(value):
    return lax.all_to_all(value, AXES, 0, 0, tiled=True)


def shards(rhs, linv, w_one, w_two, held, ranks):
    scaling = 1.0 / math.sqrt(rhs.shape[1] * PER_BLOCK)
    z, lw, msg = main_call(rhs, linv, w_one, w_two, held)
    shared = swap(pick_call(swap(msg), held))
    return last_call(shared, z, lw, held, ranks, scaling)


def solution(mesh):
    return jax.shard_map(
        shards,
        mesh=mesh,
        in_specs=(P(None, AXES), P(AXES, None, None), P(AXES, None), P(AXES, None), P(), P()),
        out_specs=P(None, AXES),
        check_vma=False,
    )
```

time: 56.1 us -> 51.8 us (0.923)
  starting transfers between devices: 3.85 us -> 0 us
  blocking collectives: 38.9 us -> 40.5 us
  Pallas kernels: 12.1 us -> 10.9 us
  waiting for transfers between devices: 0.9 us -> 0 us
    ppermute x1 -> x0, starting transfers between devices: 3.85 us -> none  [shards(): mine = mine + lax.ppermute(other, 'core', [(0, 1), (1, 0)])]
    all_to_all x3 -> x2, blocking collectives: 38.9 us -> 40.5 us  [swap(): return lax.all_to_all(value, AXES, 0, 0, tiled=True)]
    ppermute x1 -> x0, waiting for transfers between devices: 0.9 us -> none  [shards(): mine = mine + lax.ppermute(other, 'core', [(0, 1), (1, 0)])]
    pallas_call x1, Pallas kernels: 3.34 us -> 2.63 us  [last_call(): pl.pallas_call(functools.partial(last_kernel, scaling), in_specs=[pl.Bloc...]
  transfers between devices with their start and end apart: 1 -> 0, of which waited for: 1 -> 0; matrix products, arithmetic and copies ran while one was open for 0% -> 0% of each run, Pallas kernels for 0% -> 0%
where the time goes in v3:
time: 51.8 us; the launch traced here: 51.4 us
  blocking collectives  40.5 us (78%)
  Pallas kernels  10.9 us (21%)
    all_to_all x2, blocking collectives, swap(): return lax.all_to_all(value, AXES, 0, 0, tiled=True)  40.5 us
    pallas_call x1, Pallas kernels, main_call(): pl.pallas_call(main_kernel, in_specs=[pl.BlockSpec(memory_space=pltpu.HBM...  7.63 us
    pallas_call x1, Pallas kernels, last_call(): pl.pallas_call(functools.partial(last_kernel, scaling), in_specs=[pl.Bloc...  2.63 us

profile of v3, /device:TPU:1, one launch (start us, length us, event | category | flops | bytes accessed | tf_op | source)
XLA Modules:
  0.0 51.4 jit_solution(4745295396900806159)
XLA Ops:
  0.0 0.0 copy-start
  0.0 0.0 copy-start.1
  0.0 7.6 %leaves.1 = (f32[256,4096]{1,0:T(8,128)S(1)}, f32[256,4096]{1,0:T(8,128)S(1)}, f32[512,128]{1,0:T(8,128)S(1)}) custom-call(s32[16]{0:T(128)} %held.3, f32[256,4096]{1,0:T(8,128)} %rhs.1, f32[16,256,256]{2,1,0:T(8,128)} %linv.1, f32[4096,128]{1,0:T(8,128)} %w_one.1, f32[4096,128]{1,0:T(8,128)} %w_two.1), custom_call_target="tpu_custom_call" | custom-call | tf_op jit(solution)/shard_map/leaves/pallas_call | solution.py:187
  7.6 22.6 %all_to_all.22 = f32[128,4,128]{2,1,0:T(4,128)S(1)} all-to-all(f32[128,4,128]{2,1,0:T(4,128)S(1)} %bitcast.7), channel_id=1, replica_groups=mesh['clu'=8,'row'=16] {'clu','row'}, dimensions={0} | all-to-all | bytes 524288 | tf_op jit(solution)/shard_map/all_to_all | solution.py:346
  30.2 0.0 copy-done
  30.2 0.7 %pick.1 = f32[1024,128]{1,0:T(8,128)S(1)} custom-call(s32[16]{0:T(128)S(1)} %copy-done, f32[512,128]{1,0:T(8,128)S(1)} %bitcast.6), custom_call_target="tpu_custom_call" | custom-call | tf_op jit(solution)/shard_map/pick/pallas_call | solution.py:241
  30.9 17.9 %all_to_all.23 = f32[128,8,128]{2,1,0:T(8,128)S(1)} all-to-all(f32[128,8,128]{2,1,0:T(8,128)S(1)} %bitcast.4), channel_id=1, replica_groups=mesh['clu'=8,'row'=16] {'clu','row'}, dimensions={0} | all-to-all | bytes 1048576 | tf_op jit(solution)/shard_map/all_to_all | solution.py:346
  48.8 0.0 copy-done.1
  48.8 2.6 %correct.1 = f32[256,4096]{1,0:T(8,128)} custom-call(s32[16]{0:T(128)S(1)} %copy-done, s32[12]{0:T(128)S(1)} %copy-done.1, f32[1024,128]{1,0:T(8,128)S(1)} %bitcast.5, f32[256,4096]{1,0:T(8,128)S(1)} %get-tuple-element.9.z, f32[256,4096]{1,0:T(8,128)S(1)} %get-tuple-element.10.lw), custom_call_target="tpu_custom_call" | custom-call | tf_op jit(solution)/shard_map/correct/pallas_call | solution.py:330
Async XLA Ops:
  0.0 30.2 %copy-start = (s32[16]{0:T(128)S(1)}, s32[16]{0:T(128)}, u32[]{:S(2)}) copy-start(s32[16]{0:T(128)} %held.3) | copy-start | bytes 196
  0.0 48.8 %copy-start.1 = (s32[12]{0:T(128)S(1)}, s32[12]{0:T(128)}, u32[]{:S(2)}) copy-start(s32[12]{0:T(128)} %ranks.1) | copy-start | bytes 148

commit v4 on v3

--- a/solution.py
+++ b/solution.py
@@ -40,7 +40,7 @@
 
 def main_kernel(
     held_in, rhs, linv, w_one, w_two, z, lw, msg,
-    held, rhs_v, linv_v, w_v, total, even, odd, held_sem, sems,
+    held, rhs_v, linv_v, w_v, total, kept_a, kept_b, held_sem, sems,
 ):
     cols = rhs.shape[0]
     leaves, leaf, _ = linv.shape
@@ -77,16 +77,40 @@
         for copy in copies(g):
             copy.wait()
 
+    def each_pair(solve, couple):
+        wait(0)
+        solve(0, kept_a, 0)
+        solve(1, kept_a, 1)
+
+        def four(k, carry):
+            wait(2 * k + 1)
+            couple(4 * k, kept_a)
+            solve(4 * k + 2, kept_b, 0)
+            solve(4 * k + 3, kept_b, 1)
+            wait(2 * k + 2)
+            couple(4 * k + 2, kept_b)
+            solve(4 * k + 4, kept_a, 0)
+            solve(4 * k + 5, kept_a, 1)
+            return carry
+
+        lax.fori_loop(0, groups // 2 - 1, four, 0)
+        wait(groups - 1)
+        couple(leaves - 4, kept_a)
+        solve(leaves - 2, kept_b, 0)
+        solve(leaves - 1, kept_b, 1)
+        couple(leaves - 2, kept_b)
+
     def each_leaf(solve, couple):
+        even, odd = kept_a.at[0], kept_a.at[1]
         wait(0)
         solve(0, even)
 
         def pair(k, carry):
             wait(k + 1)
+            solve(2 * k + 1, odd)
             couple(2 * k, even)
-            solve(2 * k + 1, odd)
+            solve(2 * k + 2, even)
             couple(2 * k + 1, odd)
-            solve(2 * k + 2, even)
             return carry
 
         lax.fori_loop(0, groups - 1, pair, 0)
@@ -102,23 +126,27 @@
     def _():
         total[:cols] = jnp.zeros((cols, 2 * rank), jnp.float32)
 
-        def solve(i, kept):
+        def solve(i, kept, j):
             span = span_of(i)
             y = leaf_product(rhs_v[:, span], i)
             z[:, span] = y
-            kept[:cols] = y
+            kept[j, :cols] = y
 
         def couple(i, kept):
-            span = span_of(i)
-            w = jnp.concatenate([w_v[0, span, :], w_v[1, span, :]], axis=1)
-            w_high, w_low = halves(w)
+            left, right = [], []
+            for j in range(2):
+                span = span_of(i + j)
+                w = jnp.concatenate([w_v[0, span, :], w_v[1, span, :]], axis=1)
+                w_high, w_low = halves(w)
+                left.append(split3(kept[j, :cols]))
+                right += [w_high, w_low, w_high]
             total[:cols] += jnp.dot(
-                split3(kept[:cols]),
-                jnp.concatenate([w_high, w_low, w_high], axis=0),
+                jnp.concatenate(left, axis=1),
+                jnp.concatenate(right, axis=0),
                 preferred_element_type=jnp.float32,
             )
 
-        each_leaf(solve, couple)
+        each_pair(solve, couple)
         put(0, total[:half, :rank])
         put(1, total[half:cols, :rank])
         put(2, total[:half, rank:])
@@ -164,7 +192,7 @@
 
     @pl.when(position == 3)
     def _():
-        def solve(i, kept):
+        def solve(i, kept, j):
             span = span_of(i)
             x = jnp.concatenate(
                 [rhs_v[:, span], w_v[0, span, :].T, w_v[1, span, :].T], axis=0
@@ -173,7 +201,7 @@
             z[:, span] = y[:cols]
             lw[:, span] = y[cols:]
 
-        each_leaf(solve, lambda i, kept: None)
+        each_pair(solve, lambda i, kept: None)
 
 
 def main_call(rhs, linv, w_one, w_two, held):
@@ -199,8 +227,8 @@
             pltpu.VMEM((leaves, leaf, leaf), jnp.float32),
             pltpu.VMEM((2, rows, rank), jnp.float32),
             pltpu.VMEM((cols + rank, 2 * rank), jnp.float32),
-            pltpu.VMEM((cols + rank, leaf), jnp.float32),
-            pltpu.VMEM((cols + rank, leaf), jnp.float32),
+            pltpu.VMEM((2, cols + rank, leaf), jnp.float32),
+            pltpu.VMEM((2, cols + rank, leaf), jnp.float32),
             pltpu.SemaphoreType.DMA(()),
             pltpu.SemaphoreType.DMA((4, leaves // GROUP)),
         ],

time: 51.8 us -> 51.5 us (level)
  blocking collectives: 40.5 us -> 39.4 us
  Pallas kernels: 10.9 us -> 11.5 us
    all_to_all x2, blocking collectives: 40.5 us -> 39.4 us  [swap(): return lax.all_to_all(value, AXES, 0, 0, tiled=True)]
where the time goes in v4:
time: 51.5 us; the launch traced here: 50.9 us
  blocking collectives  39.4 us (77%)
  Pallas kernels  11.5 us (22%)
    all_to_all x2, blocking collectives, swap(): return lax.all_to_all(value, AXES, 0, 0, tiled=True)  39.4 us
    pallas_call x1, Pallas kernels, main_call(): pl.pallas_call(main_kernel, in_specs=[pl.BlockSpec(memory_space=pltpu.HBM...  7.85 us
    pallas_call x1, Pallas kernels, last_call(): pl.pallas_call(functools.partial(last_kernel, scaling), in_specs=[pl.Bloc...  2.97 us

profile of v4, /device:TPU:1, one launch (start us, length us, event | category | flops | bytes accessed | tf_op | source)
XLA Modules:
  0.0 50.9 jit_solution(18401868384981725906)
XLA Ops:
  0.0 0.0 copy-start
  0.0 0.0 copy-start.1
  0.0 7.9 %leaves.1 = (f32[256,4096]{1,0:T(8,128)S(1)}, f32[256,4096]{1,0:T(8,128)S(1)}, f32[512,128]{1,0:T(8,128)S(1)}) custom-call(s32[16]{0:T(128)} %held.3, f32[256,4096]{1,0:T(8,128)} %rhs.1, f32[16,256,256]{2,1,0:T(8,128)} %linv.1, f32[4096,128]{1,0:T(8,128)} %w_one.1, f32[4096,128]{1,0:T(8,128)} %w_two.1), custom_call_target="tpu_custom_call" | custom-call | tf_op jit(solution)/shard_map/leaves/pallas_call | solution.py:215
  7.9 21.5 %all_to_all.22 = f32[128,4,128]{2,1,0:T(4,128)S(1)} all-to-all(f32[128,4,128]{2,1,0:T(4,128)S(1)} %bitcast.7), channel_id=1, replica_groups=mesh['clu'=8,'row'=16] {'clu','row'}, dimensions={0} | all-to-all | bytes 524288 | tf_op jit(solution)/shard_map/all_to_all | solution.py:374
  29.4 0.0 copy-done
  29.4 0.7 %pick.1 = f32[1024,128]{1,0:T(8,128)S(1)} custom-call(s32[16]{0:T(128)S(1)} %copy-done, f32[512,128]{1,0:T(8,128)S(1)} %bitcast.6), custom_call_target="tpu_custom_call" | custom-call | tf_op jit(solution)/shard_map/pick/pallas_call | solution.py:269
  30.0 17.9 %all_to_all.23 = f32[128,8,128]{2,1,0:T(8,128)S(1)} all-to-all(f32[128,8,128]{2,1,0:T(8,128)S(1)} %bitcast.4), channel_id=1, replica_groups=mesh['clu'=8,'row'=16] {'clu','row'}, dimensions={0} | all-to-all | bytes 1048576 | tf_op jit(solution)/shard_map/all_to_all | solution.py:374
  47.9 0.0 copy-done.1
  47.9 3.0 %correct.1 = f32[256,4096]{1,0:T(8,128)} custom-call(s32[16]{0:T(128)S(1)} %copy-done, s32[12]{0:T(128)S(1)} %copy-done.1, f32[1024,128]{1,0:T(8,128)S(1)} %bitcast.5, f32[256,4096]{1,0:T(8,128)S(1)} %get-tuple-element.9.z, f32[256,4096]{1,0:T(8,128)S(1)} %get-tuple-element.10.lw), custom_call_target="tpu_custom_call" | custom-call | tf_op jit(solution)/shard_map/correct/pallas_call | solution.py:358
Async XLA Ops:
  0.0 29.4 %copy-start = (s32[16]{0:T(128)S(1)}, s32[16]{0:T(128)}, u32[]{:S(2)}) copy-start(s32[16]{0:T(128)} %held.3) | copy-start | bytes 196
  0.0 47.9 %copy-start.1 = (s32[12]{0:T(128)S(1)}, s32[12]{0:T(128)}, u32[]{:S(2)}) copy-start(s32[12]{0:T(128)} %ranks.1) | copy-start | bytes 148

commit v5 on v4

--- a/solution.py
+++ b/solution.py
@@ -152,10 +152,7 @@
         put(2, total[:half, rank:])
         put(3, total[half:cols, rank:])
 
-    @pl.when((position == 1) | (position == 2))
-    def _():
-        mine = position - 1
-        other = 2 - position
+    def middle(mine, other):
         total[...] = jnp.zeros_like(total)
 
         def solve(i, kept):
@@ -178,17 +175,17 @@
         each_leaf(solve, couple)
         summed = total[:, :rank] + total[:, rank:]
 
-        @pl.when(position == 1)
-        def _():
+        if mine == 0:
             put(0, summed[cols:])
             put(2, summed[:half])
             put(3, summed[half:cols])
-
-        @pl.when(position == 2)
-        def _():
+        else:
             put(0, summed[:half])
             put(1, summed[half:cols])
             put(2, summed[cols:])
+
+    pl.when(position == 1)(lambda: middle(0, 1))
+    pl.when(position == 2)(lambda: middle(1, 0))
 
     @pl.when(position == 3)
     def _():

time: 51.5 us -> 52.3 us (1.016)
  blocking collectives: 39.4 us -> 40.3 us
    all_to_all x2, blocking collectives: 39.4 us -> 40.3 us  [swap(): return lax.all_to_all(value, AXES, 0, 0, tiled=True)]
where the time goes in v5:
time: 52.3 us; the launch traced here: 51.8 us
  blocking collectives  40.3 us (77%)
  Pallas kernels  11.5 us (22%)
    all_to_all x2, blocking collectives, swap(): return lax.all_to_all(value, AXES, 0, 0, tiled=True)  40.3 us
    pallas_call x1, Pallas kernels, main_call(): pl.pallas_call(main_kernel, in_specs=[pl.BlockSpec(memory_space=pltpu.HBM...  7.84 us
    pallas_call x1, Pallas kernels, last_call(): pl.pallas_call(functools.partial(last_kernel, scaling), in_specs=[pl.Bloc...  2.97 us

profile of v5, /device:TPU:1, one launch (start us, length us, event | category | flops | bytes accessed | tf_op | source)
XLA Modules:
  0.0 51.8 jit_solution(6232670602957847566)
XLA Ops:
  0.0 0.0 copy-start
  0.0 0.0 copy-start.1
  0.0 7.8 %leaves.1 = (f32[256,4096]{1,0:T(8,128)S(1)}, f32[256,4096]{1,0:T(8,128)S(1)}, f32[512,128]{1,0:T(8,128)S(1)}) custom-call(s32[16]{0:T(128)} %held.3, f32[256,4096]{1,0:T(8,128)} %rhs.1, f32[16,256,256]{2,1,0:T(8,128)} %linv.1, f32[4096,128]{1,0:T(8,128)} %w_one.1, f32[4096,128]{1,0:T(8,128)} %w_two.1), custom_call_target="tpu_custom_call" | custom-call | tf_op jit(solution)/shard_map/leaves/pallas_call | solution.py:212
  7.9 22.4 %all_to_all.22 = f32[128,4,128]{2,1,0:T(4,128)S(1)} all-to-all(f32[128,4,128]{2,1,0:T(4,128)S(1)} %bitcast.7), channel_id=1, replica_groups=mesh['clu'=8,'row'=16] {'clu','row'}, dimensions={0} | all-to-all | bytes 524288 | tf_op jit(solution)/shard_map/all_to_all | solution.py:371
  30.3 0.0 copy-done
  30.3 0.7 %pick.1 = f32[1024,128]{1,0:T(8,128)S(1)} custom-call(s32[16]{0:T(128)S(1)} %copy-done, f32[512,128]{1,0:T(8,128)S(1)} %bitcast.6), custom_call_target="tpu_custom_call" | custom-call | tf_op jit(solution)/shard_map/pick/pallas_call | solution.py:266
  30.9 17.9 %all_to_all.23 = f32[128,8,128]{2,1,0:T(8,128)S(1)} all-to-all(f32[128,8,128]{2,1,0:T(8,128)S(1)} %bitcast.4), channel_id=1, replica_groups=mesh['clu'=8,'row'=16] {'clu','row'}, dimensions={0} | all-to-all | bytes 1048576 | tf_op jit(solution)/shard_map/all_to_all | solution.py:371
  48.8 0.0 copy-done.1
  48.8 3.0 %correct.1 = f32[256,4096]{1,0:T(8,128)} custom-call(s32[16]{0:T(128)S(1)} %copy-done, s32[12]{0:T(128)S(1)} %copy-done.1, f32[1024,128]{1,0:T(8,128)S(1)} %bitcast.5, f32[256,4096]{1,0:T(8,128)S(1)} %get-tuple-element.9.z, f32[256,4096]{1,0:T(8,128)S(1)} %get-tuple-element.10.lw), custom_call_target="tpu_custom_call" | custom-call | tf_op jit(solution)/shard_map/correct/pallas_call | solution.py:355
Async XLA Ops:
  0.0 30.3 %copy-start = (s32[16]{0:T(128)S(1)}, s32[16]{0:T(128)}, u32[]{:S(2)}) copy-start(s32[16]{0:T(128)} %held.3) | copy-start | bytes 196
  0.0 48.8 %copy-start.1 = (s32[12]{0:T(128)S(1)}, s32[12]{0:T(128)}, u32[]{:S(2)}) copy-start(s32[12]{0:T(128)} %ranks.1) | copy-start | bytes 148
